TPU v7x, 32 devices: a whole 2x2x4 slice. The times are simulated.
32 devices in a mesh: seq: 8 (over z, y), head: 4 (over x, core).
Axes of the slice: x: 2, y: 2, z: 4, core: 2. Of those that a mesh axis runs over, the one named last changes fastest.
Arguments:
- queries: bfloat16 [1024, 3072], P('seq', 'head'), may hold values from -2 to 2
- key_rows: bfloat16 [1024, 3072], P('seq', 'head'), may hold values from -2 to 2
- values: bfloat16 [1024, 3072], P('seq', 'head'), may hold values from -6 to 6
- conv_input: bfloat16 [1024, 3072], P('seq', 'head'), may hold values from -0.14941406 to 0.14941406
- log_gates: bfloat16 [1024, 3072], P('seq', 'head'), may hold values from -1 to 0
- grad_output: bfloat16 [1024, 3072], P('seq', 'head'), may hold values from -0.8984375 to 0.8984375
- saved_state: float32 [8, 24, 128, 128], P('seq', 'head'), may hold values from -6 to 6
- conv_kernel: float32 [4, 3072], replicated, may hold values from -3 to 3
Outputs:
- grad_queries: bfloat16 [1024, 3072], P('seq', 'head')
- grad_keys: bfloat16 [1024, 3072], P('seq', 'head')
- grad_gates: bfloat16 [1024, 3072], P('seq', 'head')
- grad_input: bfloat16 [1024, 3072], P(('seq', 'head'))
- grad_kernel: float32 [4, 3072], P(None, 'head')
All inputs are finite; a program needn't handle non-finite values.
Results may differ from a plain program's by a relative error of at most 0.0049.
Values may be sent and summed in bfloat16 or wider, within the bound.
A program may use at most 64 MiB of HBM per device.

v0:
```python
import functools

import jax
import jax.numpy as jnp
from jax import lax
from jax.experimental import pallas as pl
from jax.experimental.pallas import tpu as pltpu
from jax.sharding import PartitionSpec as P

MESH = pl.DeviceIdType.MESH
F32 = jnp.float32
BF16 = jnp.bfloat16
LANES = 128
EDGE = 16


def product(a, b, dim_a, dim_b):
    return lax.dot_general(
        a, b, (((dim_a,), (dim_b,)), ((), ())), preferred_element_type=F32
    )


def halves(x):
    high = x.astype(BF16)
    return high, (x - high.astype(F32)).astype(BF16)


def both(x, axis):
    return jnp.concatenate(halves(x), axis=axis)


def twice(x, axis):
    return jnp.concatenate([x, x], axis=axis)


def body(
    seqs, groups, inner, heads, tokens, taps,
    q_in, k_in, v_in, x_in, l_in, g_in, s_in, w_in,
    gq_out, gk_out, gg_out, gi_out, gw_out,
    q, k, v, x, l, g, s, w,
    turned, tails, c, qup, kdn, scale, ktail, terms, gk_part, gv_part, gg_part,
    push, dec, gath, dgath, alone, decays, carry, leave, ends, incoming,
    gv, gi, sums, all_sums,
    in_sem, push_s, push_r, dec_s, dec_r, hop_s, hop_r, end_s, end_r,
    edge_s, edge_r, row_s, row_r, sum_s, sum_r,
):
    p = lax.axis_index("seq")
    hd = lax.axis_index("head")
    o, i = p // inner, p % inner
    outer = seqs // inner
    part = LANES // inner
    columns = heads * LANES
    own_rows = tokens // groups
    cols = [slice(h * LANES, (h + 1) * LANES) for h in range(heads)]

    mine = pl.ds(pl.multiple_of(hd * columns, LANES), columns)
    loads = [
        pltpu.make_async_copy(src, dst, in_sem.at[n])
        for n, (src, dst) in enumerate(
            [(l_in, l), (q_in, q), (g_in, g), (k_in, k), (v_in, v), (s_in.at[0], s), (x_in, x), (w_in.at[:, mine], w)]
        )
    ]
    for load in loads:
        load.start()

    def greet(n, carried):
        pl.semaphore_signal(
            barrier, inc=1, device_id=(lax.rem(p + n, seqs), hd), device_id_type=MESH
        )
        return carried

    barrier = pltpu.get_barrier_semaphore()
    lax.fori_loop(1, seqs, greet, 0)
    for n in range(1, groups):
        pl.semaphore_signal(
            barrier, inc=1, device_id=(p, lax.rem(hd + n, groups)), device_id_type=MESH
        )

    row = lax.broadcasted_iota(jnp.int32, (tokens, tokens), 0)
    col = lax.broadcasted_iota(jnp.int32, (tokens, tokens), 1)
    lower = row >= col
    upper = col >= row
    lower_b = jnp.where(lower, 1.0, 0.0).astype(BF16)
    upper_b = jnp.where(upper, 1.0, 0.0).astype(BF16)
    strict_b = jnp.where(row > col, 1.0, 0.0).astype(BF16)

    loads[0].wait()
    total = product(lower_b, l[...], 1, 0)
    c[...] = total
    middle = total[tokens // 2 - 1 : tokens // 2]
    last = total[tokens - 1 : tokens]
    to_middle = jnp.exp(middle)
    grow = jnp.exp(total - middle)
    whole = jnp.exp(last)
    for h in range(heads):
        dec[h : h + 1] = whole[:, cols[h]]
    loads[1].wait()
    up = q[...].astype(F32) * grow
    qup[...] = up.astype(BF16)
    full = up * to_middle
    loads[2].wait()
    for h in range(heads):
        push[h] = product(twice(g[:, cols[h]], 0), both(full[:, cols[h]], 0), 0, 0).astype(BF16)

    pl.semaphore_wait(barrier, seqs - 1 + groups - 1)

    def push_copy(sender, to):
        return pltpu.make_async_remote_copy(
            src_ref=push.at[:, to * part : (to + 1) * part, :],
            dst_ref=gath.at[sender],
            send_sem=push_s.at[to],
            recv_sem=push_r.at[sender],
            device_id=(o * inner + to, hd),
            device_id_type=MESH,
        )

    def dec_copy(sender, to):
        return pltpu.make_async_remote_copy(
            src_ref=dec,
            dst_ref=dgath.at[sender],
            send_sem=dec_s.at[to],
            recv_sem=dec_r.at[sender],
            device_id=(o * inner + to, hd),
            device_id_type=MESH,
        )

    for j in range(inner):

        @pl.when(j != i)
        def _(j=j):
            push_copy(i, j).start()
            dec_copy(i, j).start()

    gath[i] = push[:, pl.ds(pl.multiple_of(i * part, part), part), :]
    dgath[i] = dec[...]

    loads[3].wait()
    loads[4].wait()
    loads[5].wait()
    total = c[...]
    middle = total[tokens // 2 - 1 : tokens // 2]
    last = total[tokens - 1 : tokens]
    down = k[...].astype(F32) * jnp.exp(middle - total)
    kdn[...] = down.astype(BF16)
    scale[...] = jnp.exp(last - total)
    ktail[...] = down * jnp.exp(last - middle)
    scores = []
    for h in range(heads):
        at = cols[h]
        g_h = g[:, at]
        score = jnp.where(lower, product(g_h, v[:, at], 1, 1), 0.0).astype(BF16)
        scores.append(score)
        total = c[:, at]
        middle = total[tokens // 2 - 1 : tokens // 2]
        from_start = product(twice(g_h, 1), both(s[h], 1), 1, 1) * jnp.exp(total)
        kdn_h = kdn[:, at]
        qup_h = qup[:, at]
        inside = product(score, kdn_h, 1, 0)
        back = product(score, qup_h, 0, 0)
        gq_out[:, at] = (jnp.exp(total - middle) * inside + from_start).astype(BF16)
        gk_part[:, at] = jnp.exp(middle - total) * back
        terms[:, at] = (
            qup_h.astype(F32) * inside - kdn_h.astype(F32) * back + q[:, at].astype(F32) * from_start
        )

    for j in range(inner):

        @pl.when(j != i)
        def _(j=j):
            push_copy(j, j).wait_recv()
            dec_copy(j, j).wait_recv()

    for h in range(heads):
        state = gath[inner - 1, h].astype(F32)
        decay = dgath[inner - 1, h : h + 1]
        for j in range(inner - 2, -1, -1):
            alone[j, h] = state
            decays[j, h] = jnp.broadcast_to(decay, (8, LANES))
            step = dgath[j, h : h + 1]
            state = gath[j, h].astype(F32) + step * state
            decay = decay * step
        alone[inner - 1, h] = state
        decays[inner - 1, h] = jnp.broadcast_to(decay, (8, LANES))

    def hop_copy():
        return pltpu.make_async_remote_copy(
            src_ref=leave,
            dst_ref=carry,
            send_sem=hop_s,
            recv_sem=hop_r,
            device_id=(p - inner, hd),
            device_id_type=MESH,
        )

    share = pl.ds(pl.multiple_of(i * part, part), part)

    def end_copy(sender, to, where):
        return pltpu.make_async_remote_copy(
            src_ref=ends.at[to],
            dst_ref=incoming.at[:, where, :],
            send_sem=end_s.at[to],
            recv_sem=end_r.at[sender],
            device_id=(o * inner + to, hd),
            device_id_type=MESH,
        )

    def hand_back():
        for h in range(heads):
            from_later = carry[h].astype(F32)
            ends[inner - 1, h] = carry[h]
            for j in range(inner - 1):
                ends[j, h] = (alone[j, h] + decays[j, h, 0:1] * from_later).astype(BF16)
        for j in range(inner):

            @pl.when(j != i)
            def _(j=j):
                end_copy(i, j, share).start()

        incoming[:, share, :] = ends[i]

    def pass_on():
        for h in range(heads):
            leave[h] = (
                alone[inner - 1, h] + decays[inner - 1, h, 0:1] * carry[h].astype(F32)
            ).astype(BF16)
        hop_copy().start()

    @pl.when(o == outer - 1)
    def _():
        carry[...] = jnp.zeros_like(carry)
        if outer > 1:
            pass_on()
        hand_back()

    for h in range(heads):
        at = cols[h]
        total = c[:, at]
        middle = total[tokens // 2 - 1 : tokens // 2]
        k_high, k_low = halves(k[:, at].astype(F32) * jnp.exp(middle - total))
        q_high, q_low = halves(q[:, at].astype(F32) * jnp.exp(total - middle))
        weight = product(
            jnp.concatenate([k_high, k_high], axis=1), jnp.concatenate([q_high, q_low], axis=1), 1, 1
        ) + product(k_low, q_high, 1, 1)
        weight = jnp.where(upper, weight, 0.0)
        gv_part[:, at] = product(both(weight, 1), twice(g[:, at], 0), 1, 0)
    gg_part[...] = product(twice(upper_b, 1), both(terms[...], 0), 1, 0)

    if outer > 1:

        @pl.when(o < outer - 1)
        def _():
            hop_copy().wait_recv()

            @pl.when(o > 0)
            def _():
                pass_on()

            hand_back()

    for h in range(heads):
        turned[h] = s[h].T
        at = cols[h]
        tail_high, tail_low = halves(ktail[:, at])
        tails[h, :, 0:LANES] = tail_high
        tails[h, :, LANES:] = tail_low

    for j in range(inner):

        @pl.when(j != i)
        def _(j=j):
            end_copy(j, j, slice(j * part, (j + 1) * part)).wait_recv()

    for h in range(heads):
        at = cols[h]
        gv[0:tokens, at] = (
            gv_part[:, at] + product(tails[h], twice(incoming[h], 1), 1, 1)
        ).astype(BF16)

    def edge_copy():
        return pltpu.make_async_remote_copy(
            src_ref=gv.at[0:EDGE],
            dst_ref=gv.at[tokens : tokens + EDGE],
            send_sem=edge_s,
            recv_sem=edge_r,
            device_id=(p - 1, hd),
            device_id_type=MESH,
        )

    @pl.when(p > 0)
    def _():
        edge_copy().start()

    @pl.when(p == seqs - 1)
    def _():
        gv[tokens : tokens + EDGE] = jnp.zeros((EDGE, columns), BF16)

    loads[6].wait()
    loads[7].wait()

    def convolve(first, end):
        rows = gv[first : end + EDGE].astype(F32)
        result = w[0:1] * rows[: end - first]
        for tap in range(1, taps):
            result = result + w[tap : tap + 1] * rows[tap : tap + end - first]
        gi[first:end] = result.astype(BF16)

    def row_copy(sender, to):
        return pltpu.make_async_remote_copy(
            src_ref=gi.at[to * own_rows : (to + 1) * own_rows],
            dst_ref=gi_out.at[:, pl.ds(pl.multiple_of(sender * columns, LANES), columns)],
            send_sem=row_s.at[to],
            recv_sem=row_r.at[sender],
            device_id=(p, to),
            device_id_type=MESH,
        )

    def keep_copy(to):
        return pltpu.make_async_copy(
            gi.at[to * own_rows : (to + 1) * own_rows], gi_out.at[:, mine], row_s.at[to]
        )

    def hand_out(to):
        @pl.when(to != hd)
        def _():
            row_copy(hd, to).start()

        @pl.when(to == hd)
        def _():
            keep_copy(to).start()

    for to in range(groups - 1):
        convolve(to * own_rows, (to + 1) * own_rows)
        hand_out(to)

    for h in range(heads):
        at = cols[h]
        later = product(v[:, at], incoming[h], 1, 0)
        gk_out[:, at] = (gk_part[:, at] + scale[:, at] * later).astype(BF16)
        own = jnp.sum(incoming[h].astype(F32) * turned[h], axis=0, keepdims=True)
        gg = (
            gg_part[:, at]
            + product(strict_b, (ktail[:, at] * later).astype(BF16), 1, 0)
            + own * dec[h : h + 1]
        )
        gg_out[:, at] = gg.astype(BF16)

    @pl.when(p < seqs - 1)
    def _():
        edge_copy().wait_recv()

    convolve((groups - 1) * own_rows, tokens)
    hand_out(groups - 1)

    rows = gv[...].astype(F32)
    x_f = x[...].astype(F32)
    for tap in range(taps):
        sums[tap : tap + 1] = jnp.sum(x_f * rows[tap : tap + tokens], axis=0, keepdims=True)

    def sum_copy(sender, to):
        return pltpu.make_async_remote_copy(
            src_ref=sums,
            dst_ref=all_sums.at[sender],
            send_sem=sum_s.at[to],
            recv_sem=sum_r.at[sender],
            device_id=(to, hd),
            device_id_type=MESH,
        )

    def send_sum(n, carried):
        sum_copy(p, lax.rem(p + n, seqs)).start()
        return carried

    lax.fori_loop(1, seqs, send_sum, 0)
    all_sums[p] = sums[...]

    def take_sum(n, carried):
        other = lax.rem(p + n, seqs)
        sum_copy(other, other).wait_recv()
        return carried

    lax.fori_loop(1, seqs, take_sum, 0)
    added = lax.fori_loop(
        0, seqs, lambda n, value: value + all_sums[n], jnp.zeros((taps, columns), F32)
    )
    gw_out[...] = added

    for sender in range(groups):

        @pl.when(sender != hd)
        def _(sender=sender):
            row_copy(sender, sender).wait_recv()

    for to in range(groups):

        @pl.when(to != hd)
        def _(to=to):
            row_copy(hd, to).wait_send()

        @pl.when(to == hd)
        def _(to=to):
            keep_copy(to).wait()

    def sent_sum(n, carried):
        sum_copy(p, lax.rem(p + n, seqs)).wait_send()
        return carried

    lax.fori_loop(1, seqs, sent_sum, 0)
    for j in range(inner):

        @pl.when(j != i)
        def _(j=j):
            push_copy(i, j).wait_send()
            dec_copy(i, j).wait_send()
            end_copy(i, j, share).wait_send()

    if outer > 1:

        @pl.when(o > 0)
        def _():
            hop_copy().wait_send()

    @pl.when(p > 0)
    def _():
        edge_copy().wait_send()


def deliver(*refs):
    count = len(refs) // 2
    copies = [
        pltpu.make_async_copy(refs[n], refs[count + n], refs[-1].at[n]) for n in range(count)
    ]
    for copy in copies:
        copy.start()
    for copy in copies:
        copy.wait()


def solution(mesh):
    seqs, groups = mesh.shape["seq"], mesh.shape["head"]
    inner = 4 if seqs % 4 == 0 else 1

    def per_device(queries, key_rows, values, conv_input, log_gates, grad_output, saved_state, conv_kernel):
        tokens, columns = queries.shape
        heads = saved_state.shape[1]
        taps = conv_kernel.shape[0]
        part = LANES // inner
        flat = (tokens, columns)
        dma = pltpu.SemaphoreType.DMA
        vmem = pltpu.VMEM
        shapes = (
            jax.ShapeDtypeStruct(flat, BF16),
            jax.ShapeDtypeStruct(flat, BF16),
            jax.ShapeDtypeStruct(flat, BF16),
            jax.ShapeDtypeStruct((tokens // groups, columns * groups), BF16),
            jax.ShapeDtypeStruct((taps, columns), F32),
        )
        results = pl.pallas_call(
            functools.partial(body, seqs, groups, inner, heads, tokens, taps),
            out_shape=tuple(vmem(made.shape, made.dtype) for made in shapes),
            in_specs=[pl.BlockSpec(memory_space=pltpu.HBM)] * 8,
            out_specs=[pl.BlockSpec(memory_space=pltpu.VMEM)] * 5,
            scratch_shapes=[vmem(flat, BF16)] * 6
            + [
                vmem((heads, LANES, LANES), F32),
                vmem((taps, columns), F32),
                vmem((heads, LANES, LANES), F32),
                vmem((heads, tokens, 2 * LANES), BF16),
                vmem(flat, F32),
                vmem(flat, BF16),
                vmem(flat, BF16),
                vmem(flat, F32),
                vmem(flat, F32),
                vmem(flat, F32),
                vmem(flat, F32),
                vmem(flat, F32),
                vmem(flat, F32),
                vmem((heads, LANES, LANES), BF16),
                vmem((heads, LANES), F32),
                vmem((inner, heads, part, LANES), BF16),
                vmem((inner, heads, LANES), F32),
                vmem((inner, heads, part, LANES), F32),
                vmem((inner, heads, 8, LANES), F32),
                vmem((heads, part, LANES), BF16),
                vmem((heads, part, LANES), BF16),
                vmem((inner, heads, part, LANES), BF16),
                vmem((heads, LANES, LANES), BF16),
                vmem((tokens + EDGE, columns), BF16),
                vmem(flat, BF16),
                vmem((taps, columns), F32),
                vmem((seqs, taps, columns), F32),
                dma((8,)),
                dma((inner,)),
                dma((inner,)),
                dma((inner,)),
                dma((inner,)),
                dma,
                dma,
                dma((inner,)),
                dma((inner,)),
                dma,
                dma,
                dma((groups,)),
                dma((groups,)),
                dma((seqs,)),
                dma((seqs,)),
            ],
            compiler_params=pltpu.CompilerParams(
                collective_id=0, has_side_effects=True, vmem_limit_bytes=60 * 1024 * 1024
            ),
        )(queries, key_rows, values, conv_input, log_gates, grad_output, saved_state, conv_kernel)
        return pl.pallas_call(
            deliver,
            out_shape=shapes,
            in_specs=[pl.BlockSpec(memory_space=pltpu.VMEM)] * len(shapes),
            out_specs=[pl.BlockSpec(memory_space=pltpu.HBM)] * len(shapes),
            scratch_shapes=[dma((len(shapes),))],
        )(*results)

    return jax.shard_map(
        per_device,
        mesh=mesh,
        in_specs=(
            P("seq", "head"),
            P("seq", "head"),
            P("seq", "head"),
            P("seq", "head"),
            P("seq", "head"),
            P("seq", "head"),
            P("seq", "head", None, None),
            P(),
        ),
        out_specs=(
            P("seq", "head"),
            P("seq", "head"),
            P("seq", "head"),
            P(("seq", "head"), None),
            P(None, "head"),
        ),
        check_vma=False,
    )
```

profile of v0, /device:TPU:0, one launch (start us, length us, event | category | flops | bytes accessed | tf_op | source)
XLA Modules:
  0.0 31.0 jit_solution(14852222404813284535)
XLA Ops:
  0.6 25.0 %shard_map.119 = (bf16[128,768]{1,0:T(8,128)(2,1)S(1)}, bf16[128,768]{1,0:T(8,128)(2,1)S(1)}, bf16[128,768]{1,0:T(8,128)(2,1)S(1)}, bf16[32,3072]{1,0:T(8,128)(2,1)S(1)}, f32[4,768]{1,0:T(4,128)S(1)}) custom-call(bf16[128,768]{1,0:T(8,128)(2,1)} %q_in.1, bf16[128,768]{1,0:T(8,128)(2,1)} %k_in.1, bf16[128,768]{1,0:T(8,128)(2,1)} %v_in.1, ...), custom_call_target="tpu_custom_call" | custom-call | tf_op jit(solution)/shard_map/pallas_call | solution.py:457
  25.6 0.0 copy-start
  25.6 0.7 %copy-done = bf16[128,768]{1,0:T(8,128)(2,1)} copy-done((bf16[128,768]{1,0:T(8,128)(2,1)}, bf16[128,768]{1,0:T(8,128)(2,1)S(1)}, u32[]{:S(2)}) %copy-start) | copy-done | bytes 196632
  26.3 0.0 copy-start.1
  26.3 0.7 %copy-done.1 = bf16[128,768]{1,0:T(8,128)(2,1)} copy-done((bf16[128,768]{1,0:T(8,128)(2,1)}, bf16[128,768]{1,0:T(8,128)(2,1)S(1)}, u32[]{:S(2)}) %copy-start.1) | copy-done | bytes 196632
  26.9 0.0 copy-start.2
  26.9 0.7 %copy-done.2 = bf16[128,768]{1,0:T(8,128)(2,1)} copy-done((bf16[128,768]{1,0:T(8,128)(2,1)}, bf16[128,768]{1,0:T(8,128)(2,1)S(1)}, u32[]{:S(2)}) %copy-start.2) | copy-done | bytes 196632
  27.6 0.0 copy-start.3
  27.6 0.7 %copy-done.3 = bf16[32,3072]{1,0:T(8,128)(2,1)} copy-done((bf16[32,3072]{1,0:T(8,128)(2,1)}, bf16[32,3072]{1,0:T(8,128)(2,1)S(1)}, u32[]{:S(2)}) %copy-start.3) | copy-done | bytes 196632
  28.3 0.0 copy-start.4
  28.3 0.6 %copy-done.4 = f32[4,768]{1,0:T(4,128)} copy-done((f32[4,768]{1,0:T(4,128)}, f32[4,768]{1,0:T(4,128)S(1)}, u32[]{:S(2)}) %copy-start.4) | copy-done | bytes 12312
  28.9 2.1 %shard_map.120 = (bf16[128,768]{1,0:T(8,128)(2,1)}, bf16[128,768]{1,0:T(8,128)(2,1)}, bf16[128,768]{1,0:T(8,128)(2,1)}, bf16[32,3072]{1,0:T(8,128)(2,1)}, f32[4,768]{1,0:T(4,128)}) custom-call(bf16[128,768]{1,0:T(8,128)(2,1)} %copy-done, bf16[128,768]{1,0:T(8,128)(2,1)} %copy-done.1, bf16[128,768]{1,0:T(8,128)(2,1)} %copy-done.2, ...), custom_call_target="tpu_custom_call" | custom-call | tf_op jit(solution)/shard_map/pallas_call | solution.py:511
Async XLA Ops:
  25.6 0.7 %copy-start = (bf16[128,768]{1,0:T(8,128)(2,1)}, bf16[128,768]{1,0:T(8,128)(2,1)S(1)}, u32[]{:S(2)}) copy-start(bf16[128,768]{1,0:T(8,128)(2,1)S(1)} %get-tuple-element.10.refs_0_) | copy-start | bytes 589828
  26.3 0.7 %copy-start.1 = (bf16[128,768]{1,0:T(8,128)(2,1)}, bf16[128,768]{1,0:T(8,128)(2,1)S(1)}, u32[]{:S(2)}) copy-start(bf16[128,768]{1,0:T(8,128)(2,1)S(1)} %get-tuple-element.11.refs_1_) | copy-start | bytes 589828
  26.9 0.7 %copy-start.2 = (bf16[128,768]{1,0:T(8,128)(2,1)}, bf16[128,768]{1,0:T(8,128)(2,1)S(1)}, u32[]{:S(2)}) copy-start(bf16[128,768]{1,0:T(8,128)(2,1)S(1)} %get-tuple-element.12.refs_2_) | copy-start | bytes 589828
  27.6 0.7 %copy-start.3 = (bf16[32,3072]{1,0:T(8,128)(2,1)}, bf16[32,3072]{1,0:T(8,128)(2,1)S(1)}, u32[]{:S(2)}) copy-start(bf16[32,3072]{1,0:T(8,128)(2,1)S(1)} %get-tuple-element.13.refs_3_) | copy-start | bytes 589828
  28.3 0.6 %copy-start.4 = (f32[4,768]{1,0:T(4,128)}, f32[4,768]{1,0:T(4,128)S(1)}, u32[]{:S(2)}) copy-start(f32[4,768]{1,0:T(4,128)S(1)} %get-tuple-element.14.refs_4_) | copy-start | bytes 36868
where the time goes:
time: 31.2 us; the launch traced here: 31 us
  Pallas kernels  27.1 us (87%)
  local copies, waits for them, and re-layouts  3.28 us (11%)
  between operations  0.65 us (2%)
    pallas_call x1, Pallas kernels, per_device(): pl.pallas_call(functools.partial(body, seqs, groups, inner, heads, tokens...  25 us
    unnamed x10, local copies, waits for them, and re-layouts  3.28 us
    pallas_call x1, Pallas kernels, per_device(): pl.pallas_call(deliver, out_shape=shapes, in_specs=[pl.BlockSpec(memory_s...  2.13 us

commit v1 on v0

--- a/solution.py
+++ b/solution.py
@@ -42,7 +42,7 @@
     push, dec, gath, dgath, alone, decays, carry, leave, ends, incoming,
     gv, gi, sums, all_sums,
     in_sem, push_s, push_r, dec_s, dec_r, hop_s, hop_r, end_s, end_r,
-    edge_s, edge_r, row_s, row_r, sum_s, sum_r,
+    before_s, before_r, edge_s, edge_r, row_s, row_r, sum_s, sum_r,
 ):
     p = lax.axis_index("seq")
     hd = lax.axis_index("head")
@@ -51,13 +51,15 @@
     part = LANES // inner
     columns = heads * LANES
     own_rows = tokens // groups
+    half = heads // 2
+    chunks = [(0, half), (half, heads)] if half else [(0, heads)]
     cols = [slice(h * LANES, (h + 1) * LANES) for h in range(heads)]
 
     mine = pl.ds(pl.multiple_of(hd * columns, LANES), columns)
     loads = [
         pltpu.make_async_copy(src, dst, in_sem.at[n])
         for n, (src, dst) in enumerate(
-            [(l_in, l), (q_in, q), (g_in, g), (k_in, k), (v_in, v), (s_in.at[0], s), (x_in, x), (w_in.at[:, mine], w)]
+            [(l_in, l), (q_in, q), (g_in, g), (k_in, k), (v_in, v), (s_in.at[0], s), (x_in, x.at[EDGE:]), (w_in.at[:, mine], w)]
         )
     ]
     for load in loads:
@@ -99,17 +101,14 @@
     qup[...] = up.astype(BF16)
     full = up * to_middle
     loads[2].wait()
-    for h in range(heads):
-        push[h] = product(twice(g[:, cols[h]], 0), both(full[:, cols[h]], 0), 0, 0).astype(BF16)
-
-    pl.semaphore_wait(barrier, seqs - 1 + groups - 1)
-
-    def push_copy(sender, to):
-        return pltpu.make_async_remote_copy(
-            src_ref=push.at[:, to * part : (to + 1) * part, :],
-            dst_ref=gath.at[sender],
-            send_sem=push_s.at[to],
-            recv_sem=push_r.at[sender],
+
+    def push_copy(n, sender, to):
+        first, end = chunks[n]
+        return pltpu.make_async_remote_copy(
+            src_ref=push.at[first:end, to * part : (to + 1) * part, :],
+            dst_ref=gath.at[sender, first:end],
+            send_sem=push_s.at[n, to],
+            recv_sem=push_r.at[n, sender],
             device_id=(o * inner + to, hd),
             device_id_type=MESH,
         )
@@ -124,12 +123,40 @@
             device_id_type=MESH,
         )
 
-    for j in range(inner):
-
-        @pl.when(j != i)
-        def _(j=j):
-            push_copy(i, j).start()
-            dec_copy(i, j).start()
+    def before_copy():
+        return pltpu.make_async_remote_copy(
+            src_ref=x.at[tokens : tokens + EDGE],
+            dst_ref=x.at[0:EDGE],
+            send_sem=before_s,
+            recv_sem=before_r,
+            device_id=(p + 1, hd),
+            device_id_type=MESH,
+        )
+
+    for n, (first, end) in enumerate(chunks):
+        for h in range(first, end):
+            push[h] = product(
+                twice(g[:, cols[h]], 0), both(full[:, cols[h]], 0), 0, 0
+            ).astype(BF16)
+        if n == 0:
+            pl.semaphore_wait(barrier, seqs - 1 + groups - 1)
+        for j in range(inner):
+
+            @pl.when(j != i)
+            def _(j=j):
+                if n == 0:
+                    dec_copy(i, j).start()
+                push_copy(n, i, j).start()
+
+    loads[6].wait()
+
+    @pl.when(p < seqs - 1)
+    def _():
+        before_copy().start()
+
+    @pl.when(p == 0)
+    def _():
+        x[0:EDGE] = jnp.zeros((EDGE, columns), BF16)
 
     gath[i] = push[:, pl.ds(pl.multiple_of(i * part, part), part), :]
     dgath[i] = dec[...]
@@ -163,49 +190,40 @@
             qup_h.astype(F32) * inside - kdn_h.astype(F32) * back + q[:, at].astype(F32) * from_start
         )
 
-    for j in range(inner):
-
-        @pl.when(j != i)
-        def _(j=j):
-            push_copy(j, j).wait_recv()
-            dec_copy(j, j).wait_recv()
-
-    for h in range(heads):
-        state = gath[inner - 1, h].astype(F32)
-        decay = dgath[inner - 1, h : h + 1]
-        for j in range(inner - 2, -1, -1):
-            alone[j, h] = state
-            decays[j, h] = jnp.broadcast_to(decay, (8, LANES))
-            step = dgath[j, h : h + 1]
-            state = gath[j, h].astype(F32) + step * state
-            decay = decay * step
-        alone[inner - 1, h] = state
-        decays[inner - 1, h] = jnp.broadcast_to(decay, (8, LANES))
-
-    def hop_copy():
-        return pltpu.make_async_remote_copy(
-            src_ref=leave,
-            dst_ref=carry,
-            send_sem=hop_s,
-            recv_sem=hop_r,
+    share = pl.ds(pl.multiple_of(i * part, part), part)
+
+    def hop_copy(n):
+        first, end = chunks[n]
+        return pltpu.make_async_remote_copy(
+            src_ref=leave.at[first:end],
+            dst_ref=carry.at[first:end],
+            send_sem=hop_s.at[n],
+            recv_sem=hop_r.at[n],
             device_id=(p - inner, hd),
             device_id_type=MESH,
         )
 
-    share = pl.ds(pl.multiple_of(i * part, part), part)
-
-    def end_copy(sender, to, where):
-        return pltpu.make_async_remote_copy(
-            src_ref=ends.at[to],
-            dst_ref=incoming.at[:, where, :],
-            send_sem=end_s.at[to],
-            recv_sem=end_r.at[sender],
+    def end_copy(n, sender, to, where):
+        first, end = chunks[n]
+        return pltpu.make_async_remote_copy(
+            src_ref=ends.at[to, first:end],
+            dst_ref=incoming.at[first:end, where, :],
+            send_sem=end_s.at[n, to],
+            recv_sem=end_r.at[n, sender],
             device_id=(o * inner + to, hd),
             device_id_type=MESH,
         )
 
-    def hand_back():
-        for h in range(heads):
+    def pass_on(n):
+        for h in range(*chunks[n]):
+            leave[h] = (
+                alone[inner - 1, h] + decays[inner - 1, h, 0:1] * carry[h].astype(F32)
+            ).astype(BF16)
+        hop_copy(n).start()
+
+    def hand_back(n):
+        first, end = chunks[n]
+        for h in range(first, end):
             from_later = carry[h].astype(F32)
             ends[inner - 1, h] = carry[h]
             for j in range(inner - 1):
@@ -214,23 +232,40 @@
 
             @pl.when(j != i)
             def _(j=j):
-                end_copy(i, j, share).start()
-
-        incoming[:, share, :] = ends[i]
-
-    def pass_on():
-        for h in range(heads):
-            leave[h] = (
-                alone[inner - 1, h] + decays[inner - 1, h, 0:1] * carry[h].astype(F32)
-            ).astype(BF16)
-        hop_copy().start()
+                end_copy(n, i, j, share).start()
+
+        incoming[first:end, share, :] = ends[i, first:end]
 
     @pl.when(o == outer - 1)
     def _():
         carry[...] = jnp.zeros_like(carry)
-        if outer > 1:
-            pass_on()
-        hand_back()
+
+    for n, (first, end) in enumerate(chunks):
+        for j in range(inner):
+
+            @pl.when(j != i)
+            def _(j=j):
+                if n == 0:
+                    dec_copy(j, j).wait_recv()
+                push_copy(n, j, j).wait_recv()
+
+        for h in range(first, end):
+            state = gath[inner - 1, h].astype(F32)
+            decay = dgath[inner - 1, h : h + 1]
+            for j in range(inner - 2, -1, -1):
+                alone[j, h] = state
+                decays[j, h] = jnp.broadcast_to(decay, (8, LANES))
+                step = dgath[j, h : h + 1]
+                state = gath[j, h].astype(F32) + step * state
+                decay = decay * step
+            alone[inner - 1, h] = state
+            decays[inner - 1, h] = jnp.broadcast_to(decay, (8, LANES))
+
+        @pl.when(o == outer - 1)
+        def _(n=n):
+            if outer > 1:
+                pass_on(n)
+            hand_back(n)
 
     for h in range(heads):
         at = cols[h]
@@ -249,13 +284,14 @@
 
         @pl.when(o < outer - 1)
         def _():
-            hop_copy().wait_recv()
-
-            @pl.when(o > 0)
-            def _():
-                pass_on()
-
-            hand_back()
+            for n in range(len(chunks)):
+                hop_copy(n).wait_recv()
+
+                @pl.when(o > 0)
+                def _(n=n):
+                    pass_on(n)
+
+                hand_back(n)
 
     for h in range(heads):
         turned[h] = s[h].T
@@ -264,17 +300,18 @@
         tails[h, :, 0:LANES] = tail_high
         tails[h, :, LANES:] = tail_low
 
-    for j in range(inner):
-
-        @pl.when(j != i)
-        def _(j=j):
-            end_copy(j, j, slice(j * part, (j + 1) * part)).wait_recv()
-
-    for h in range(heads):
-        at = cols[h]
-        gv[0:tokens, at] = (
-            gv_part[:, at] + product(tails[h], twice(incoming[h], 1), 1, 1)
-        ).astype(BF16)
+    for n, (first, end) in enumerate(chunks):
+        for j in range(inner):
+
+            @pl.when(j != i)
+            def _(j=j):
+                end_copy(n, j, j, slice(j * part, (j + 1) * part)).wait_recv()
+
+        for h in range(first, end):
+            at = cols[h]
+            gv[0:tokens, at] = (
+                gv_part[:, at] + product(tails[h], twice(incoming[h], 1), 1, 1)
+            ).astype(BF16)
 
     def edge_copy():
         return pltpu.make_async_remote_copy(
@@ -289,12 +326,36 @@
     @pl.when(p > 0)
     def _():
         edge_copy().start()
+        before_copy().wait_recv()
 
     @pl.when(p == seqs - 1)
     def _():
         gv[tokens : tokens + EDGE] = jnp.zeros((EDGE, columns), BF16)
 
-    loads[6].wait()
+    rows = gv[0:tokens].astype(F32)
+    x_f = x[...].astype(F32)
+    for tap in range(taps):
+        sums[tap : tap + 1] = jnp.sum(
+            rows * x_f[EDGE - tap : EDGE - tap + tokens], axis=0, keepdims=True
+        )
+
+    def sum_copy(sender, to):
+        return pltpu.make_async_remote_copy(
+            src_ref=sums,
+            dst_ref=all_sums.at[sender],
+            send_sem=sum_s.at[to],
+            recv_sem=sum_r.at[sender],
+            device_id=(to, hd),
+            device_id_type=MESH,
+        )
+
+    def send_sum(n, carried):
+        sum_copy(p, lax.rem(p + n, seqs)).start()
+        return carried
+
+    lax.fori_loop(1, seqs, send_sum, 0)
+    all_sums[p] = sums[...]
+
     loads[7].wait()
 
     def convolve(first, end):
@@ -351,27 +412,6 @@
     convolve((groups - 1) * own_rows, tokens)
     hand_out(groups - 1)
 
-    rows = gv[...].astype(F32)
-    x_f = x[...].astype(F32)
-    for tap in range(taps):
-        sums[tap : tap + 1] = jnp.sum(x_f * rows[tap : tap + tokens], axis=0, keepdims=True)
-
-    def sum_copy(sender, to):
-        return pltpu.make_async_remote_copy(
-            src_ref=sums,
-            dst_ref=all_sums.at[sender],
-            send_sem=sum_s.at[to],
-            recv_sem=sum_r.at[sender],
-            device_id=(to, hd),
-            device_id_type=MESH,
-        )
-
-    def send_sum(n, carried):
-        sum_copy(p, lax.rem(p + n, seqs)).start()
-        return carried
-
-    lax.fori_loop(1, seqs, send_sum, 0)
-    all_sums[p] = sums[...]
 
     def take_sum(n, carried):
         other = lax.rem(p + n, seqs)
@@ -409,19 +449,25 @@
 
         @pl.when(j != i)
         def _(j=j):
-            push_copy(i, j).wait_send()
             dec_copy(i, j).wait_send()
-            end_copy(i, j, share).wait_send()
+            for n in range(len(chunks)):
+                push_copy(n, i, j).wait_send()
+                end_copy(n, i, j, share).wait_send()
 
     if outer > 1:
 
         @pl.when(o > 0)
         def _():
-            hop_copy().wait_send()
+            for n in range(len(chunks)):
+                hop_copy(n).wait_send()
 
     @pl.when(p > 0)
     def _():
         edge_copy().wait_send()
+
+    @pl.when(p < seqs - 1)
+    def _():
+        before_copy().wait_send()
 
 
 def deliver(*refs):
@@ -459,7 +505,9 @@
             out_shape=tuple(vmem(made.shape, made.dtype) for made in shapes),
             in_specs=[pl.BlockSpec(memory_space=pltpu.HBM)] * 8,
             out_specs=[pl.BlockSpec(memory_space=pltpu.VMEM)] * 5,
-            scratch_shapes=[vmem(flat, BF16)] * 6
+            scratch_shapes=[vmem(flat, BF16)] * 3
+            + [vmem((tokens + EDGE, columns), BF16)]
+            + [vmem(flat, BF16)] * 2
             + [
                 vmem((heads, LANES, LANES), F32),
                 vmem((taps, columns), F32),
@@ -489,14 +537,16 @@
                 vmem((taps, columns), F32),
                 vmem((seqs, taps, columns), F32),
                 dma((8,)),
+                dma((2, inner)),
+                dma((2, inner)),
                 dma((inner,)),
                 dma((inner,)),
-                dma((inner,)),
-                dma((inner,)),
+                dma((2,)),
+                dma((2,)),
+                dma((2, inner)),
+                dma((2, inner)),
                 dma,
                 dma,
-                dma((inner,)),
-                dma((inner,)),
                 dma,
                 dma,
                 dma((groups,)),

time: 31.2 us -> 28.9 us (0.926)
  Pallas kernels: 27.1 us -> 24.8 us
    pallas_call x1, Pallas kernels: 25 us -> 22.7 us  [per_device(): pl.pallas_call(functools.partial(body, seqs, groups, inner, heads, tokens...]
where the time goes in v1:
time: 28.9 us; the launch traced here: 28.8 us
  Pallas kernels  24.8 us (86%)
  local copies, waits for them, and re-layouts  3.28 us (11%)
  between operations  0.65 us (2%)
    pallas_call x1, Pallas kernels, per_device(): pl.pallas_call(functools.partial(body, seqs, groups, inner, heads, tokens...  22.7 us
    unnamed x10, local copies, waits for them, and re-layouts  3.28 us
    pallas_call x1, Pallas kernels, per_device(): pl.pallas_call(deliver, out_shape=shapes, in_specs=[pl.BlockSpec(memory_s...  2.13 us

profile of v1, /device:TPU:0, one launch (start us, length us, event | category | flops | bytes accessed | tf_op | source)
XLA Modules:
  0.0 28.8 jit_solution(6709632159766581287)
XLA Ops:
  0.6 22.7 %shard_map.119 = (bf16[128,768]{1,0:T(8,128)(2,1)S(1)}, bf16[128,768]{1,0:T(8,128)(2,1)S(1)}, bf16[128,768]{1,0:T(8,128)(2,1)S(1)}, bf16[32,3072]{1,0:T(8,128)(2,1)S(1)}, f32[4,768]{1,0:T(4,128)S(1)}) custom-call(bf16[128,768]{1,0:T(8,128)(2,1)} %q_in.1, bf16[128,768]{1,0:T(8,128)(2,1)} %k_in.1, bf16[128,768]{1,0:T(8,128)(2,1)} %v_in.1, ...), custom_call_target="tpu_custom_call" | custom-call | tf_op jit(solution)/shard_map/pallas_call | solution.py:503
  23.3 0.0 copy-start
  23.3 0.7 %copy-done = bf16[128,768]{1,0:T(8,128)(2,1)} copy-done((bf16[128,768]{1,0:T(8,128)(2,1)}, bf16[128,768]{1,0:T(8,128)(2,1)S(1)}, u32[]{:S(2)}) %copy-start) | copy-done | bytes 196632
  24.0 0.0 copy-start.1
  24.0 0.7 %copy-done.1 = bf16[128,768]{1,0:T(8,128)(2,1)} copy-done((bf16[128,768]{1,0:T(8,128)(2,1)}, bf16[128,768]{1,0:T(8,128)(2,1)S(1)}, u32[]{:S(2)}) %copy-start.1) | copy-done | bytes 196632
  24.7 0.0 copy-start.2
  24.7 0.7 %copy-done.2 = bf16[128,768]{1,0:T(8,128)(2,1)} copy-done((bf16[128,768]{1,0:T(8,128)(2,1)}, bf16[128,768]{1,0:T(8,128)(2,1)S(1)}, u32[]{:S(2)}) %copy-start.2) | copy-done | bytes 196632
  25.4 0.0 copy-start.3
  25.4 0.7 %copy-done.3 = bf16[32,3072]{1,0:T(8,128)(2,1)} copy-done((bf16[32,3072]{1,0:T(8,128)(2,1)}, bf16[32,3072]{1,0:T(8,128)(2,1)S(1)}, u32[]{:S(2)}) %copy-start.3) | copy-done | bytes 196632
  26.0 0.0 copy-start.4
  26.0 0.6 %copy-done.4 = f32[4,768]{1,0:T(4,128)} copy-done((f32[4,768]{1,0:T(4,128)}, f32[4,768]{1,0:T(4,128)S(1)}, u32[]{:S(2)}) %copy-start.4) | copy-done | bytes 12312
  26.6 2.1 %shard_map.120 = (bf16[128,768]{1,0:T(8,128)(2,1)}, bf16[128,768]{1,0:T(8,128)(2,1)}, bf16[128,768]{1,0:T(8,128)(2,1)}, bf16[32,3072]{1,0:T(8,128)(2,1)}, f32[4,768]{1,0:T(4,128)}) custom-call(bf16[128,768]{1,0:T(8,128)(2,1)} %copy-done, bf16[128,768]{1,0:T(8,128)(2,1)} %copy-done.1, bf16[128,768]{1,0:T(8,128)(2,1)} %copy-done.2, ...), custom_call_target="tpu_custom_call" | custom-call | tf_op jit(solution)/shard_map/pallas_call | solution.py:561
Async XLA Ops:
  23.3 0.7 %copy-start = (bf16[128,768]{1,0:T(8,128)(2,1)}, bf16[128,768]{1,0:T(8,128)(2,1)S(1)}, u32[]{:S(2)}) copy-start(bf16[128,768]{1,0:T(8,128)(2,1)S(1)} %get-tuple-element.10.refs_0_) | copy-start | bytes 589828
  24.0 0.7 %copy-start.1 = (bf16[128,768]{1,0:T(8,128)(2,1)}, bf16[128,768]{1,0:T(8,128)(2,1)S(1)}, u32[]{:S(2)}) copy-start(bf16[128,768]{1,0:T(8,128)(2,1)S(1)} %get-tuple-element.11.refs_1_) | copy-start | bytes 589828
  24.7 0.7 %copy-start.2 = (bf16[128,768]{1,0:T(8,128)(2,1)}, bf16[128,768]{1,0:T(8,128)(2,1)S(1)}, u32[]{:S(2)}) copy-start(bf16[128,768]{1,0:T(8,128)(2,1)S(1)} %get-tuple-element.12.refs_2_) | copy-start | bytes 589828
  25.4 0.7 %copy-start.3 = (bf16[32,3072]{1,0:T(8,128)(2,1)}, bf16[32,3072]{1,0:T(8,128)(2,1)S(1)}, u32[]{:S(2)}) copy-start(bf16[32,3072]{1,0:T(8,128)(2,1)S(1)} %get-tuple-element.13.refs_3_) | copy-start | bytes 589828
  26.0 0.6 %copy-start.4 = (f32[4,768]{1,0:T(4,128)}, f32[4,768]{1,0:T(4,128)S(1)}, u32[]{:S(2)}) copy-start(f32[4,768]{1,0:T(4,128)S(1)} %get-tuple-element.14.refs_4_) | copy-start | bytes 36868

commit v2 on v1

--- a/solution.py
+++ b/solution.py
@@ -564,6 +564,7 @@
             in_specs=[pl.BlockSpec(memory_space=pltpu.VMEM)] * len(shapes),
             out_specs=[pl.BlockSpec(memory_space=pltpu.HBM)] * len(shapes),
             scratch_shapes=[dma((len(shapes),))],
+            compiler_params=pltpu.CompilerParams(vmem_limit_bytes=2 * 1024 * 1024),
         )(*results)
 
     return jax.shard_map(

time: 28.9 us -> 24.4 us (0.84)
  local copies, waits for them, and re-layouts: 3.28 us -> 0 us
  Pallas kernels: 24.8 us -> 23.6 us
    unnamed x10 -> x0, local copies, waits for them, and re-layouts: 3.28 us -> none
    pallas_call x1, Pallas kernels: 2.13 us -> 0.92 us  [per_device(): pl.pallas_call(deliver, out_shape=shapes, in_specs=[pl.BlockSpec(memory_s...]
where the time goes in v2:
time: 24.4 us; the launch traced here: 24.3 us
  Pallas kernels  23.6 us (97%)
  between operations  0.64 us (3%)
    pallas_call x1, Pallas kernels, per_device(): pl.pallas_call(functools.partial(body, seqs, groups, inner, heads, tokens...  22.7 us
    pallas_call x1, Pallas kernels, per_device(): pl.pallas_call(deliver, out_shape=shapes, in_specs=[pl.BlockSpec(memory_s...  0.92 us

profile of v2, /device:TPU:0, one launch (start us, length us, event | category | flops | bytes accessed | tf_op | source)
XLA Modules:
  0.0 24.3 jit_solution(18359001211044497400)
XLA Ops:
  0.6 22.7 %shard_map.119 = (bf16[128,768]{1,0:T(8,128)(2,1)S(1)}, bf16[128,768]{1,0:T(8,128)(2,1)S(1)}, bf16[128,768]{1,0:T(8,128)(2,1)S(1)}, bf16[32,3072]{1,0:T(8,128)(2,1)S(1)}, f32[4,768]{1,0:T(4,128)S(1)}) custom-call(bf16[128,768]{1,0:T(8,128)(2,1)} %q_in.1, bf16[128,768]{1,0:T(8,128)(2,1)} %k_in.1, bf16[128,768]{1,0:T(8,128)(2,1)} %v_in.1, ...), custom_call_target="tpu_custom_call" | custom-call | tf_op jit(solution)/shard_map/pallas_call | solution.py:503
  23.3 0.9 %shard_map.120 = (bf16[128,768]{1,0:T(8,128)(2,1)}, bf16[128,768]{1,0:T(8,128)(2,1)}, bf16[128,768]{1,0:T(8,128)(2,1)}, bf16[32,3072]{1,0:T(8,128)(2,1)}, f32[4,768]{1,0:T(4,128)}) custom-call(bf16[128,768]{1,0:T(8,128)(2,1)S(1)} %get-tuple-element.10.refs_0_, bf16[128,768]{1,0:T(8,128)(2,1)S(1)} %get-tuple-element.11.refs_1_, ...), custom_call_target="tpu_custom_call" | custom-call | tf_op jit(solution)/shard_map/pallas_call | solution.py:561

commit v3 on v2

--- a/solution.py
+++ b/solution.py
@@ -31,6 +31,12 @@
 
 def twice(x, axis):
     return jnp.concatenate([x, x], axis=axis)
+
+
+def spans(heads):
+    count = 3 if heads % 3 == 0 else 1
+    width = heads // count
+    return [(n * width, (n + 1) * width) for n in range(count)]
 
 
 def body(
@@ -52,7 +58,7 @@
     columns = heads * LANES
     own_rows = tokens // groups
     half = heads // 2
-    chunks = [(0, half), (half, heads)] if half else [(0, heads)]
+    chunks = spans(heads)
     cols = [slice(h * LANES, (h + 1) * LANES) for h in range(heads)]
 
     mine = pl.ds(pl.multiple_of(hd * columns, LANES), columns)
@@ -148,16 +154,6 @@
                     dec_copy(i, j).start()
                 push_copy(n, i, j).start()
 
-    loads[6].wait()
-
-    @pl.when(p < seqs - 1)
-    def _():
-        before_copy().start()
-
-    @pl.when(p == 0)
-    def _():
-        x[0:EDGE] = jnp.zeros((EDGE, columns), BF16)
-
     gath[i] = push[:, pl.ds(pl.multiple_of(i * part, part), part), :]
     dgath[i] = dec[...]
 
@@ -171,12 +167,11 @@
     kdn[...] = down.astype(BF16)
     scale[...] = jnp.exp(last - total)
     ktail[...] = down * jnp.exp(last - middle)
-    scores = []
-    for h in range(heads):
+
+    def inside_block(h):
         at = cols[h]
         g_h = g[:, at]
         score = jnp.where(lower, product(g_h, v[:, at], 1, 1), 0.0).astype(BF16)
-        scores.append(score)
         total = c[:, at]
         middle = total[tokens // 2 - 1 : tokens // 2]
         from_start = product(twice(g_h, 1), both(s[h], 1), 1, 1) * jnp.exp(total)
@@ -190,6 +185,10 @@
             qup_h.astype(F32) * inside - kdn_h.astype(F32) * back + q[:, at].astype(F32) * from_start
         )
 
+
+    for h in range(half):
+        inside_block(h)
+
     share = pl.ds(pl.multiple_of(i * part, part), part)
 
     def hop_copy(n):
@@ -267,7 +266,7 @@
                 pass_on(n)
             hand_back(n)
 
-    for h in range(heads):
+    def values_part(h):
         at = cols[h]
         total = c[:, at]
         middle = total[tokens // 2 - 1 : tokens // 2]
@@ -278,7 +277,21 @@
         ) + product(k_low, q_high, 1, 1)
         weight = jnp.where(upper, weight, 0.0)
         gv_part[:, at] = product(both(weight, 1), twice(g[:, at], 0), 1, 0)
-    gg_part[...] = product(twice(upper_b, 1), both(terms[...], 0), 1, 0)
+
+    loads[6].wait()
+
+    @pl.when(p < seqs - 1)
+    def _():
+        before_copy().start()
+
+    @pl.when(p == 0)
+    def _():
+        x[0:EDGE] = jnp.zeros((EDGE, columns), BF16)
+
+    for h in range(half, heads):
+        inside_block(h)
+    for h in range(half):
+        values_part(h)
 
     if outer > 1:
 
@@ -293,6 +306,8 @@
 
                 hand_back(n)
 
+    for h in range(half, heads):
+        values_part(h)
     for h in range(heads):
         turned[h] = s[h].T
         at = cols[h]
@@ -393,6 +408,7 @@
         convolve(to * own_rows, (to + 1) * own_rows)
         hand_out(to)
 
+    gg_part[...] = product(twice(upper_b, 1), both(terms[...], 0), 1, 0)
     for h in range(heads):
         at = cols[h]
         later = product(v[:, at], incoming[h], 1, 0)
@@ -537,14 +553,14 @@
                 vmem((taps, columns), F32),
                 vmem((seqs, taps, columns), F32),
                 dma((8,)),
-                dma((2, inner)),
-                dma((2, inner)),
+                dma((len(spans(heads)), inner)),
+                dma((len(spans(heads)), inner)),
                 dma((inner,)),
                 dma((inner,)),
-                dma((2,)),
-                dma((2,)),
-                dma((2, inner)),
-                dma((2, inner)),
+                dma((len(spans(heads)),)),
+                dma((len(spans(heads)),)),
+                dma((len(spans(heads)), inner)),
+                dma((len(spans(heads)), inner)),
                 dma,
                 dma,
                 dma,

time: 24.4 us -> 24.2 us (level)
  no operation moved by 1% of the time
where the time goes in v3:
time: 24.2 us; the launch traced here: 24.1 us
  Pallas kernels  23.4 us (97%)
  between operations  0.64 us (3%)
    pallas_call x1, Pallas kernels, per_device(): pl.pallas_call(functools.partial(body, seqs, groups, inner, heads, tokens...  22.5 us
    pallas_call x1, Pallas kernels, per_device(): pl.pallas_call(deliver, out_shape=shapes, in_specs=[pl.BlockSpec(memory_s...  0.92 us

profile of v3, /device:TPU:0, one launch (start us, length us, event | category | flops | bytes accessed | tf_op | source)
XLA Modules:
  0.0 24.1 jit_solution(9994874209666223675)
XLA Ops:
  0.6 22.5 %shard_map.119 = (bf16[128,768]{1,0:T(8,128)(2,1)S(1)}, bf16[128,768]{1,0:T(8,128)(2,1)S(1)}, bf16[128,768]{1,0:T(8,128)(2,1)S(1)}, bf16[32,3072]{1,0:T(8,128)(2,1)S(1)}, f32[4,768]{1,0:T(4,128)S(1)}) custom-call(bf16[128,768]{1,0:T(8,128)(2,1)} %q_in.1, bf16[128,768]{1,0:T(8,128)(2,1)} %k_in.1, bf16[128,768]{1,0:T(8,128)(2,1)} %v_in.1, ...), custom_call_target="tpu_custom_call" | custom-call | tf_op jit(solution)/shard_map/pallas_call | solution.py:519
  23.2 0.9 %shard_map.120 = (bf16[128,768]{1,0:T(8,128)(2,1)}, bf16[128,768]{1,0:T(8,128)(2,1)}, bf16[128,768]{1,0:T(8,128)(2,1)}, bf16[32,3072]{1,0:T(8,128)(2,1)}, f32[4,768]{1,0:T(4,128)}) custom-call(bf16[128,768]{1,0:T(8,128)(2,1)S(1)} %get-tuple-element.10.refs_0_, bf16[128,768]{1,0:T(8,128)(2,1)S(1)} %get-tuple-element.11.refs_1_, ...), custom_call_target="tpu_custom_call" | custom-call | tf_op jit(solution)/shard_map/pallas_call | solution.py:577

commit v4 on v3

--- a/solution.py
+++ b/solution.py
@@ -46,9 +46,9 @@
     q, k, v, x, l, g, s, w,
     turned, tails, c, qup, kdn, scale, ktail, terms, gk_part, gv_part, gg_part,
     push, dec, gath, dgath, alone, decays, carry, leave, ends, incoming,
-    gv, gi, sums, all_sums,
+    gv, gi, sums, all_sums, group_sum, group_sums,
     in_sem, push_s, push_r, dec_s, dec_r, hop_s, hop_r, end_s, end_r,
-    before_s, before_r, edge_s, edge_r, row_s, row_r, sum_s, sum_r,
+    before_s, before_r, edge_s, edge_r, row_s, row_r, sum_s, sum_r, total_s, total_r,
 ):
     p = lax.axis_index("seq")
     hd = lax.axis_index("head")
@@ -360,16 +360,27 @@
             dst_ref=all_sums.at[sender],
             send_sem=sum_s.at[to],
             recv_sem=sum_r.at[sender],
-            device_id=(to, hd),
-            device_id_type=MESH,
-        )
-
-    def send_sum(n, carried):
-        sum_copy(p, lax.rem(p + n, seqs)).start()
-        return carried
-
-    lax.fori_loop(1, seqs, send_sum, 0)
-    all_sums[p] = sums[...]
+            device_id=(o * inner + to, hd),
+            device_id_type=MESH,
+        )
+
+    def total_copy(sender, to):
+        return pltpu.make_async_remote_copy(
+            src_ref=group_sum,
+            dst_ref=group_sums.at[sender],
+            send_sem=total_s.at[to],
+            recv_sem=total_r.at[sender],
+            device_id=(to * inner + i, hd),
+            device_id_type=MESH,
+        )
+
+    for j in range(inner):
+
+        @pl.when(j != i)
+        def _(j=j):
+            sum_copy(i, j).start()
+
+    all_sums[i] = sums[...]
 
     loads[7].wait()
 
@@ -409,7 +420,8 @@
         hand_out(to)
 
     gg_part[...] = product(twice(upper_b, 1), both(terms[...], 0), 1, 0)
-    for h in range(heads):
+
+    def keys_and_gates(h):
         at = cols[h]
         later = product(v[:, at], incoming[h], 1, 0)
         gk_out[:, at] = (gk_part[:, at] + scale[:, at] * later).astype(BF16)
@@ -421,6 +433,9 @@
         )
         gg_out[:, at] = gg.astype(BF16)
 
+    for h in range(half):
+        keys_and_gates(h)
+
     @pl.when(p < seqs - 1)
     def _():
         edge_copy().wait_recv()
@@ -429,15 +444,34 @@
     hand_out(groups - 1)
 
 
-    def take_sum(n, carried):
-        other = lax.rem(p + n, seqs)
-        sum_copy(other, other).wait_recv()
-        return carried
-
-    lax.fori_loop(1, seqs, take_sum, 0)
-    added = lax.fori_loop(
-        0, seqs, lambda n, value: value + all_sums[n], jnp.zeros((taps, columns), F32)
-    )
+    for j in range(inner):
+
+        @pl.when(j != i)
+        def _(j=j):
+            sum_copy(j, j).wait_recv()
+
+    added = all_sums[0]
+    for j in range(1, inner):
+        added = added + all_sums[j]
+    group_sum[...] = added
+    for n in range(outer):
+
+        @pl.when(n != o)
+        def _(n=n):
+            total_copy(o, n).start()
+
+    group_sums[o] = added
+    for h in range(half, heads):
+        keys_and_gates(h)
+    for n in range(outer):
+
+        @pl.when(n != o)
+        def _(n=n):
+            total_copy(n, n).wait_recv()
+
+    added = group_sums[0]
+    for n in range(1, outer):
+        added = added + group_sums[n]
     gw_out[...] = added
 
     for sender in range(groups):
@@ -456,16 +490,18 @@
         def _(to=to):
             keep_copy(to).wait()
 
-    def sent_sum(n, carried):
-        sum_copy(p, lax.rem(p + n, seqs)).wait_send()
-        return carried
-
-    lax.fori_loop(1, seqs, sent_sum, 0)
+    for n in range(outer):
+
+        @pl.when(n != o)
+        def _(n=n):
+            total_copy(o, n).wait_send()
+
     for j in range(inner):
 
         @pl.when(j != i)
         def _(j=j):
             dec_copy(i, j).wait_send()
+            sum_copy(i, j).wait_send()
             for n in range(len(chunks)):
                 push_copy(n, i, j).wait_send()
                 end_copy(n, i, j, share).wait_send()
@@ -551,7 +587,9 @@
                 vmem((tokens + EDGE, columns), BF16),
                 vmem(flat, BF16),
                 vmem((taps, columns), F32),
-                vmem((seqs, taps, columns), F32),
+                vmem((inner, taps, columns), F32),
+                vmem((taps, columns), F32),
+                vmem((seqs // inner, taps, columns), F32),
                 dma((8,)),
                 dma((len(spans(heads)), inner)),
                 dma((len(spans(heads)), inner)),
@@ -567,8 +605,10 @@
                 dma,
                 dma((groups,)),
                 dma((groups,)),
-                dma((seqs,)),
-                dma((seqs,)),
+                dma((inner,)),
+                dma((inner,)),
+                dma((seqs // inner,)),
+                dma((seqs // inner,)),
             ],
             compiler_params=pltpu.CompilerParams(
                 collective_id=0, has_side_effects=True, vmem_limit_bytes=60 * 1024 * 1024

time: 24.2 us -> 24 us (level)
  no operation moved by 1% of the time
where the time goes in v4:
time: 24 us; the launch traced here: 23.9 us
  Pallas kernels  23.2 us (97%)
  between operations  0.64 us (3%)
    pallas_call x1, Pallas kernels, per_device(): pl.pallas_call(functools.partial(body, seqs, groups, inner, heads, tokens...  22.3 us
    pallas_call x1, Pallas kernels, per_device(): pl.pallas_call(deliver, out_shape=shapes, in_specs=[pl.BlockSpec(memory_s...  0.92 us

profile of v4, /device:TPU:0, one launch (start us, length us, event | category | flops | bytes accessed | tf_op | source)
XLA Modules:
  0.0 23.9 jit_solution(10182313166206572480)
XLA Ops:
  0.6 22.3 %shard_map.119 = (bf16[128,768]{1,0:T(8,128)(2,1)S(1)}, bf16[128,768]{1,0:T(8,128)(2,1)S(1)}, bf16[128,768]{1,0:T(8,128)(2,1)S(1)}, bf16[32,3072]{1,0:T(8,128)(2,1)S(1)}, f32[4,768]{1,0:T(4,128)S(1)}) custom-call(bf16[128,768]{1,0:T(8,128)(2,1)} %q_in.1, bf16[128,768]{1,0:T(8,128)(2,1)} %k_in.1, bf16[128,768]{1,0:T(8,128)(2,1)} %v_in.1, ...), custom_call_target="tpu_custom_call" | custom-call | tf_op jit(solution)/shard_map/pallas_call | solution.py:555
  23.0 0.9 %shard_map.120 = (bf16[128,768]{1,0:T(8,128)(2,1)}, bf16[128,768]{1,0:T(8,128)(2,1)}, bf16[128,768]{1,0:T(8,128)(2,1)}, bf16[32,3072]{1,0:T(8,128)(2,1)}, f32[4,768]{1,0:T(4,128)}) custom-call(bf16[128,768]{1,0:T(8,128)(2,1)S(1)} %get-tuple-element.10.refs_0_, bf16[128,768]{1,0:T(8,128)(2,1)S(1)} %get-tuple-element.11.refs_1_, ...), custom_call_target="tpu_custom_call" | custom-call | tf_op jit(solution)/shard_map/pallas_call | solution.py:617

commit v5 on v4

--- a/solution.py
+++ b/solution.py
@@ -260,11 +260,11 @@
             alone[inner - 1, h] = state
             decays[inner - 1, h] = jnp.broadcast_to(decay, (8, LANES))
 
-        @pl.when(o == outer - 1)
-        def _(n=n):
-            if outer > 1:
+        if outer > 1:
+
+            @pl.when(o == outer - 1)
+            def _(n=n):
                 pass_on(n)
-            hand_back(n)
 
     def values_part(h):
         at = cols[h]
@@ -278,18 +278,14 @@
         weight = jnp.where(upper, weight, 0.0)
         gv_part[:, at] = product(both(weight, 1), twice(g[:, at], 0), 1, 0)
 
-    loads[6].wait()
-
-    @pl.when(p < seqs - 1)
-    def _():
-        before_copy().start()
-
-    @pl.when(p == 0)
-    def _():
-        x[0:EDGE] = jnp.zeros((EDGE, columns), BF16)
-
     for h in range(half, heads):
         inside_block(h)
+
+    @pl.when(o == outer - 1)
+    def _():
+        for n in range(len(chunks)):
+            hand_back(n)
+
     for h in range(half):
         values_part(h)
 
@@ -305,6 +301,16 @@
                     pass_on(n)
 
                 hand_back(n)
+
+    loads[6].wait()
+
+    @pl.when(p < seqs - 1)
+    def _():
+        before_copy().start()
+
+    @pl.when(p == 0)
+    def _():
+        x[0:EDGE] = jnp.zeros((EDGE, columns), BF16)
 
     for h in range(half, heads):
         values_part(h)

time: 24 us -> 24.1 us (level)
  no operation moved by 1% of the time
where the time goes in v5:
time: 24.1 us; the launch traced here: 23.9 us
  Pallas kernels  23.3 us (97%)
  between operations  0.64 us (3%)
    pallas_call x1, Pallas kernels, per_device(): pl.pallas_call(functools.partial(body, seqs, groups, inner, heads, tokens...  22.4 us
    pallas_call x1, Pallas kernels, per_device(): pl.pallas_call(deliver, out_shape=shapes, in_specs=[pl.BlockSpec(memory_s...  0.92 us

profile of v5, /device:TPU:0, one launch (start us, length us, event | category | flops | bytes accessed | tf_op | source)
XLA Modules:
  0.0 23.9 jit_solution(12664077485013135915)
XLA Ops:
  0.6 22.4 %shard_map.119 = (bf16[128,768]{1,0:T(8,128)(2,1)S(1)}, bf16[128,768]{1,0:T(8,128)(2,1)S(1)}, bf16[128,768]{1,0:T(8,128)(2,1)S(1)}, bf16[32,3072]{1,0:T(8,128)(2,1)S(1)}, f32[4,768]{1,0:T(4,128)S(1)}) custom-call(bf16[128,768]{1,0:T(8,128)(2,1)} %q_in.1, bf16[128,768]{1,0:T(8,128)(2,1)} %k_in.1, bf16[128,768]{1,0:T(8,128)(2,1)} %v_in.1, ...), custom_call_target="tpu_custom_call" | custom-call | tf_op jit(solution)/shard_map/pallas_call | solution.py:561
  23.0 0.9 %shard_map.120 = (bf16[128,768]{1,0:T(8,128)(2,1)}, bf16[128,768]{1,0:T(8,128)(2,1)}, bf16[128,768]{1,0:T(8,128)(2,1)}, bf16[32,3072]{1,0:T(8,128)(2,1)}, f32[4,768]{1,0:T(4,128)}) custom-call(bf16[128,768]{1,0:T(8,128)(2,1)S(1)} %get-tuple-element.10.refs_0_, bf16[128,768]{1,0:T(8,128)(2,1)S(1)} %get-tuple-element.11.refs_1_, ...), custom_call_target="tpu_custom_call" | custom-call | tf_op jit(solution)/shard_map/pallas_call | solution.py:623
